TPU v7x, 256 devices: a whole 4x4x8 slice. The times are simulated.
256 devices in a mesh: mem: 8 (over z_hi, x), reg: 32 (over y, z_lo, core).
Axes of the slice: x: 4, y: 4, z: 8 (z_hi: 2, z_lo: 4; z = z_hi * 4 + z_lo), core: 2. Of those that a mesh axis runs over, the one named last changes fastest.
Arguments:
- ensemble: bfloat16 [256, 8, 16384], P('mem', None, 'reg'), may hold values from -6 to 6
- conv_first: bfloat16 [2, 9, 8, 64], replicated, may hold values from -0.75 to 0.75
- bias_first: float32 [2, 64], replicated, may hold values from -3 to 3
- conv_second: bfloat16 [2, 9, 64, 8], replicated, may hold values from -0.25 to 0.25
- bias_second: float32 [2, 8], replicated, may hold values from -3 to 3
- observed_cell: int32 [64, 16, 32], P('reg', 'mem'), may hold values from 0 to 127
- observed_value: float32 [64, 16, 32], P('reg', 'mem'), may hold values from -8 to 8
- observed_precision: float32 [64, 16, 32], P('reg', 'mem'), may hold values from 0.25 to 4
Outputs:
- analysis: bfloat16 [256, 8, 16384], P('mem', None, 'reg')
All inputs are finite; a program needn't handle non-finite values. Where the computation divides by a largest or mean magnitude, that divisor is 1e-20 or more.
Results may differ from a plain program's by a relative error of at most 0.0079.
Values may be sent and summed in bfloat16 or wider, within the bound.
A program may use at most 64 MiB of HBM per device.

v0:
```python
import functools

import jax
import jax.numpy as jnp
from jax import lax
from jax.experimental import pallas as pl
from jax.experimental.pallas import tpu as pltpu
from jax.sharding import PartitionSpec as P

K = 256
C = 8
HID = 64
NMEM = 8
NREG = 32
MEM_DEV = 32
NPC = 16
BF = jnp.bfloat16
F32 = jnp.float32
NEAR = [(dr, dm) for dr in (-1, 0, 1) for dm in (-1, 0, 1)]
TOP, BOTTOM = 4, 5


def dot(a, b):
    return lax.dot_general(a, b, (((1,), (0,)), ((), ())), preferred_element_type=F32)


def dot_nt(a, b):
    return lax.dot_general(a, b, (((1,), (1,)), ((), ())), preferred_element_type=F32)


def iota(shape, dim):
    return lax.broadcasted_iota(jnp.int32, shape, dim)


def block_swap(arrays):
    block = iota(arrays[0].shape, 1) // 16
    for step in (1, 2, 4):
        high = (block & step) != 0
        swapped = list(arrays)
        for a in range(8):
            if a & step:
                continue
            b = a | step
            swapped[a] = jnp.where(high, pltpu.roll(arrays[b], 16 * step, 1), arrays[a])
            swapped[b] = jnp.where(high, arrays[b], pltpu.roll(arrays[a], 128 - 16 * step, 1))
        arrays = swapped
    return arrays


def cell_order(inverse):
    plain, tiled = iota((256, 256), 1 if inverse else 0), iota((256, 256), 0 if inverse else 1)
    source = ((tiled // 4) % 4) * 64 + (tiled // 16) * 4 + tiled % 4
    return jnp.where(plain == source, 1.0, 0.0).astype(BF)


def strips_of(taps, flip):
    zero = jnp.zeros((C, HID), F32)
    strips = {}
    for row_step in (-1, 0, 1):
        for col in range(-1, 5):
            pieces = []
            for j in range(4):
                step = j - col if flip else col - j
                pieces.append(taps[3 * (row_step + 1) + step + 1] if abs(step) <= 1 else zero)
            strips[row_step, col] = jnp.concatenate(pieces, axis=1)
    return strips


def build_weights(taps, flip, raw, base):
    strips = strips_of(taps, flip)
    for tile in range(6):
        for row in range(4):
            if flip:
                hidden_row = {TOP: -1, BOTTOM: 4}.get(tile, tile)
                step = hidden_row - row
            else:
                step = {TOP: row - 4, BOTTOM: row + 4 - 3}.get(tile, row - tile)
            if abs(step) > 1:
                continue
            for side in (0, 1):
                for j in range(4):
                    col = j
                    if side:
                        col = {0: 4, 3: -1}.get(j)
                    if col is None:
                        continue
                    rows = pl.ds(4 * row + j, C, stride=16)
                    raw[base + tile, side, 0, rows, :] = strips[step, col][:, 0:128]
                    raw[base + tile, side, 1, rows, :] = strips[step, col][:, 128:256]


def kernel(
    ens_ref,
    first_ref,
    bias_a_ref,
    second_ref,
    bias_b_ref,
    cell_ref,
    value_ref,
    prec_ref,
    out_ref,
    raw,
    w_a,
    w_b,
    field,
    wide,
    hid,
    rel,
    rel_b,
    send_tiles,
    members,
    near,
    local,
    decay,
    send_back,
    back,
    halo_send,
    halo_recv,
    tile_send,
    tile_recv,
    near_send,
    near_recv,
    back_send,
    back_recv,
):
    m = lax.axis_index("mem")
    r = lax.axis_index("reg")
    barrier = pltpu.get_barrier_semaphore()

    def inside(dr, dm):
        return (r + dr >= 0) & (r + dr < NREG) & (m + dm >= 0) & (m + dm < NMEM)

    def peer(d):
        return lax.rem(m + d, NMEM)

    for d in range(1, NMEM):
        pl.semaphore_signal(
            barrier, inc=1, device_id={"mem": peer(d), "reg": r}, device_id_type=pl.DeviceIdType.MESH
        )
    arrivals = jnp.int32(NMEM - 1)
    for dr, dm in NEAR:
        if dr == 0:
            continue

        @pl.when(inside(dr, dm))
        def _(dr=dr, dm=dm):
            pl.semaphore_signal(
                barrier,
                inc=1,
                device_id={"mem": m + dm, "reg": r + dr},
                device_id_type=pl.DeviceIdType.MESH,
            )

        arrivals = arrivals + jnp.where(inside(dr, dm), 1, 0)

    order = cell_order(False)
    for p in range(2):
        cells = dot(ens_ref[:, 256 * p : 256 * p + 256], order)
        rel[0] = cells[:, 0:128]
        rel[1] = cells[:, 128:256]
        for half in range(2):
            channels = [rel[half, pl.ds(c, MEM_DEV, stride=C), :] for c in range(C)]
            for q, tile in enumerate(block_swap(channels)):
                field[0, 1 + p, 1 + 8 * half + q] = tile.astype(BF)
    edge = jnp.zeros((MEM_DEV, 128), BF)
    for f in range(2):
        for p in range(4):
            field[f, p, 0] = edge
            field[f, p, NPC + 1] = edge

    @pl.when(r == 0)
    def _():
        field[0, 0, 1 : NPC + 1] = jnp.zeros((NPC, MEM_DEV, 128), BF)

    @pl.when(r == NREG - 1)
    def _():
        field[0, 3, 1 : NPC + 1] = jnp.zeros((NPC, MEM_DEV, 128), BF)

    for slot, (dr, dm) in enumerate(NEAR):
        if (dr, dm) == (0, 0):
            continue

        @pl.when(jnp.logical_not(inside(dr, dm)))
        def _(slot=slot):
            near[slot] = jnp.zeros((K + 16, 128), BF)

    pl.semaphore_wait(barrier, arrivals)

    def halo_copy(down):
        return pltpu.make_async_remote_copy(
            src_ref=field.at[0, 2 if down else 1, pl.ds(1, NPC)],
            dst_ref=field.at[0, 0 if down else 3, pl.ds(1, NPC)],
            send_sem=halo_send.at[1 if down else 0],
            recv_sem=halo_recv.at[1 if down else 0],
            device_id={"mem": m, "reg": r + 1 if down else r - 1},
            device_id_type=pl.DeviceIdType.MESH,
        )

    @pl.when(r < NREG - 1)
    def _():
        halo_copy(True).start()

    @pl.when(r > 0)
    def _():
        halo_copy(False).start()

    raw[...] = jnp.zeros(raw.shape, F32)
    unit = jnp.where(iota((C, C), 0) == iota((C, C), 1), 1.0, 0.0).astype(BF)
    for f in range(2):
        taps = [
            0.5 * first_ref[pl.ds((9 * f + t) * C, C), :].astype(F32) for t in range(9)
        ]
        build_weights(taps, False, raw, 12 * f)
        turned = dot_nt(unit, second_ref[pl.ds(9 * HID * f, 9 * HID), :])
        taps = [turned[:, HID * t : HID * t + HID] for t in range(9)]
        build_weights(taps, True, raw, 12 * f + 6)
        for tile in range(6):
            for side in range(2):
                span = slice(128 * side, 128 * side + 128)
                for part in range(2):
                    lanes = slice(128 * part, 128 * part + 128)
                    w_a[f, tile, span, lanes] = raw[12 * f + tile, side, part].astype(BF)
                    w_b[f, tile, lanes, span] = jnp.transpose(
                        raw[12 * f + 6 + tile, side, part]
                    ).astype(BF)

    lane = iota((1, 128), 1)
    for target in range(4):
        for slot, (dr, dm) in enumerate(NEAR):
            a = 2 * dr + lane // 64 - target // 2
            b = 2 * dm + (lane // 32) % 2 - target % 2
            keep = (jnp.abs(a) <= 2) & (jnp.abs(b) <= 2) & inside(dr, dm)
            fall = jnp.exp((a * a + b * b).astype(F32) * (-1.0 / 9.0))
            decay[target, slot : slot + 1, :] = jnp.where(keep, fall, 0.0)

    row_lane = iota((1, 1, 128), 2)
    bias_lane = iota((1, 128), 1)
    keep_top = jnp.where(r == 0, 0.0, 1.0).astype(F32)
    keep_bottom = jnp.where(r == NREG - 1, 0.0, 1.0).astype(F32)
    keep = (keep_top, None, None, keep_bottom)

    def widen(f, p):
        right = field[f, p, 2 : NPC + 2].astype(F32)
        left = field[f, p, 0:NPC].astype(F32)
        side = jnp.where(row_lane % 4 < 2, right, left).astype(BF)
        wide[p, :, 0:128] = field[f, p, 1 : NPC + 1].reshape(NPC * MEM_DEV, 128)
        wide[p, :, 128:256] = side.reshape(NPC * MEM_DEV, 128)

    def hidden(f, p, i, bias):
        total = dot(wide[p], w_a[f, i])
        if i == 0:
            total = total + dot(wide[p - 1], w_a[f, TOP])
        if i == 3:
            total = total + dot(wide[p + 1], w_a[f, BOTTOM])
        total = total + bias
        total = total + total * jnp.tanh(total)
        if keep[p] is not None:
            total = total * keep[p]
        hid[p, i] = total.astype(BF)

    def branch(f, p, bias):
        total = None
        terms = [(p, i, i) for i in range(4)] + [(p - 1, 3, TOP), (p + 1, 0, BOTTOM)]
        if p == 0:
            terms = [(0, 1, 1), (0, 2, 2), (0, 3, 3), (1, 0, BOTTOM)]
        if p == 3:
            terms = [(3, 0, 0), (3, 1, 1), (3, 2, 2), (2, 3, TOP)]
        for hp, hi, tile in terms:
            part = dot(hid[hp, hi], w_b[f, tile])
            total = part if total is None else total + part
        own = total[:, 0:128].reshape(NPC, MEM_DEV, 128)
        side = total[:, 128:256].reshape(NPC, MEM_DEV, 128)
        none = jnp.zeros((1, MEM_DEV, 128), F32)
        before = jnp.concatenate([none, side[: NPC - 1]], axis=0)
        after = jnp.concatenate([side[1:], none], axis=0)
        moved = jnp.where(row_lane % 4 < 2, before, after)
        result = field[f, p, 1 : NPC + 1].astype(F32) + (own + moved + bias[None])
        if keep[p] is not None:
            result = result * keep[p]
        return result.astype(BF)

    def biases(f):
        half = 0.5 * bias_a_ref[f : f + 1, :]
        first = jnp.concatenate([half] * 4, axis=1)
        second = jnp.zeros((1, 128), F32)
        for c in range(C):
            second = jnp.where(bias_lane // 16 == c, bias_b_ref[f : f + 1, c : c + 1], second)
        return first, second

    bias_a, bias_b = biases(0)
    widen(0, 1)
    widen(0, 2)
    for p, i in ((1, 1), (1, 2), (2, 1), (2, 2), (1, 3), (2, 0)):
        hidden(0, p, i, bias_a)

    @pl.when(r < NREG - 1)
    def _():
        halo_copy(False).wait_recv()

    @pl.when(r > 0)
    def _():
        halo_copy(True).wait_recv()

    widen(0, 0)
    widen(0, 3)
    for p, i in ((1, 0), (2, 3), (0, 1), (0, 2), (0, 3), (3, 0), (3, 1), (3, 2)):
        hidden(0, p, i, bias_a)
    for p in range(4):
        field[1, p, 1 : NPC + 1] = branch(0, p, bias_b)

    bias_a, bias_b = biases(1)
    for p in range(4):
        widen(1, p)
    hidden(1, 0, 3, bias_a)
    hidden(1, 3, 0, bias_a)
    for p in (1, 2):
        for i in range(4):
            hidden(1, p, i, bias_a)
    for p in (1, 2):
        tiles = branch(1, p, bias_b).reshape(NMEM, 2, MEM_DEV, 128)
        for ql in range(2):
            send_tiles[:, 2 * (p - 1) + ql] = tiles[:, ql]

    def exchange(d, source, target, send_sem, recv_sem):
        return pltpu.make_async_remote_copy(
            src_ref=source.at[peer(d)],
            dst_ref=target.at[m],
            send_sem=send_sem.at[d],
            recv_sem=recv_sem.at[d],
            device_id={"mem": peer(d), "reg": r},
            device_id_type=pl.DeviceIdType.MESH,
        )

    tile_copies = [exchange(d, send_tiles, members, tile_send, tile_recv) for d in range(1, NMEM)]
    for copy in tile_copies:
        copy.start()
    members[m] = send_tiles[m]
    for copy in tile_copies:
        copy.wait_recv()

    def row_of(ref):
        return jnp.concatenate([ref[t // 2, t % 2 : t % 2 + 1, :] for t in range(4)], axis=1)

    cells = row_of(cell_ref)
    root = jnp.sqrt(row_of(prec_ref))
    picker = jnp.where(iota((128, 128), 0) == cells, 1.0, 0.0).astype(BF)
    seen = jnp.zeros((K, 128), F32)
    for t in range(4):
        tile = members[:, t].reshape(K, 128)
        seen = jnp.where(lane // 32 == t, dot(tile, picker), seen)
    seen_center = jnp.sum(seen, axis=0, keepdims=True) * (1.0 / K)
    near[4, 0:K] = ((seen - seen_center) * root).astype(BF)
    depart = (row_of(value_ref) - seen_center) * root
    depart_high = depart.astype(BF).astype(F32)
    depart_low = depart - depart_high
    sub = iota((16, 128), 0)
    near[4, K : K + 16] = jnp.where(
        sub == 0, depart_high, jnp.where(sub == 1, depart_low, 0.0)
    ).astype(BF)

    def near_copy(slot):
        dr, dm = NEAR[slot]
        return pltpu.make_async_remote_copy(
            src_ref=near.at[4],
            dst_ref=near.at[8 - slot],
            send_sem=near_send.at[slot],
            recv_sem=near_recv.at[8 - slot],
            device_id={"mem": m + dm, "reg": r + dr},
            device_id_type=pl.DeviceIdType.MESH,
        )

    for slot, (dr, dm) in enumerate(NEAR):
        if slot == 4:
            continue

        @pl.when(inside(dr, dm))
        def _(slot=slot):
            near_copy(slot).start()

    centers = []
    for t in range(4):
        tile = members[:, t].reshape(K, 128).astype(F32)
        centers.append(jnp.sum(tile, axis=0, keepdims=True) * (1.0 / K))

    for slot, (dr, dm) in enumerate(NEAR):
        if slot == 4:
            continue

        @pl.when(inside(dr, dm))
        def _(slot=slot):
            near_copy(8 - slot).wait_recv()

    summed = jnp.zeros((K, 8), F32)
    for slot in range(9):
        block = near[slot, 0:K].astype(F32)
        tail = near[slot, K : K + 16].astype(F32)
        depart = tail[0:1] + tail[1:2]
        pulls = []
        for t in range(4):
            fall = decay[t, slot : slot + 1, :]
            local[t, :, 128 * slot : 128 * slot + 128] = (block * fall).astype(BF)
            pulls.append(fall * fall * depart)
        pulls = jnp.concatenate(pulls, axis=0)
        high = pulls.astype(BF).astype(F32)
        both = jnp.concatenate([high, pulls - high], axis=0).astype(BF)
        summed = summed + dot_nt(near[slot, 0:K], both)

    eye = iota((K, K), 0) == iota((K, K), 1)
    for t in range(4):
        system = dot_nt(local[t], local[t]) + jnp.where(eye, float(K - 1), 0.0)
        rows = jnp.sum(jnp.abs(system), axis=0, keepdims=True)
        bound = jnp.max(rows, axis=1, keepdims=True)
        scale = 1.0 / bound
        a_mat = system * scale
        a_bf = a_mat.astype(BF)
        y = 1.5 * a_mat - 0.5 * dot(a_bf, a_bf)
        c = 1.5
        d_mat = -0.5 * a_mat
        for _ in range(2):
            y_bf = y.astype(BF)
            d_bf = d_mat.astype(BF)
            m_mat = c * y + dot(d_bf, y_bf)
            m_bf = m_mat.astype(BF)
            y = 1.5 * y - 0.5 * dot(y_bf, m_bf)
            d_mat = 1.5 * d_mat - (0.5 * c) * m_mat - 0.5 * dot(m_bf, d_bf)
            c = 1.5 * c
        y_bf = y.astype(BF)
        d_bf = d_mat.astype(BF)
        spread = members[:, t].reshape(K, 128).astype(F32) - centers[t]
        pull = summed[:, t : t + 1] + summed[:, 4 + t : 5 + t]
        x = jnp.concatenate([spread, jnp.broadcast_to(pull, (K, 128))], axis=1)
        g = c * x + dot(d_bf, x.astype(BF))
        h = dot(y_bf, g.astype(BF))
        g = 1.5 * g - 0.5 * (c * h + dot(d_bf, h.astype(BF)))
        shift = jnp.sum(g[:, 0:128] * g[:, 128:256], axis=0, keepdims=True) * scale
        final = centers[t] + shift + jnp.sqrt(float(K - 1) * scale) * g[:, 0:128]
        send_back[:, t] = final.astype(BF).reshape(NMEM, MEM_DEV, 128)

    back_copies = [exchange(d, send_back, back, back_send, back_recv) for d in range(1, NMEM)]
    for copy in back_copies:
        copy.start()
    back[m] = send_back[m]
    for copy in back_copies:
        copy.wait_recv()

    order = cell_order(True)
    for p in range(2):
        for half in range(2):
            tiles = [
                back[4 * half + q // 2, 2 * p + q % 2].astype(F32) for q in range(8)
            ]
            for c, channel in enumerate(block_swap(tiles)):
                rel_b[half, pl.ds(c, MEM_DEV, stride=C), :] = channel
        cells = jnp.concatenate([rel_b[0], rel_b[1]], axis=1).astype(BF)
        out_ref[:, 256 * p : 256 * p + 256] = dot(cells, order).astype(BF)

    @pl.when(r < NREG - 1)
    def _():
        halo_copy(True).wait_send()

    @pl.when(r > 0)
    def _():
        halo_copy(False).wait_send()

    for copy in tile_copies:
        copy.wait_send()
    for slot, (dr, dm) in enumerate(NEAR):
        if slot == 4:
            continue

        @pl.when(inside(dr, dm))
        def _(slot=slot):
            near_copy(slot).wait_send()

    for copy in back_copies:
        copy.wait_send()


def body(
    ensemble,
    conv_first,
    bias_first,
    conv_second,
    bias_second,
    observed_cell,
    observed_value,
    observed_precision,
):
    vmem = pl.BlockSpec(memory_space=pltpu.VMEM)
    rows = NPC * MEM_DEV
    result = pl.pallas_call(
        kernel,
        out_shape=jax.ShapeDtypeStruct((MEM_DEV * C, 512), BF),
        in_specs=[vmem] * 8,
        out_specs=vmem,
        scratch_shapes=[
            pltpu.VMEM((24, 2, 2, 128, 128), F32),
            pltpu.VMEM((2, 6, 256, 256), BF),
            pltpu.VMEM((2, 6, 256, 256), BF),
            pltpu.VMEM((2, 4, NPC + 2, MEM_DEV, 128), BF),
            pltpu.VMEM((4, rows, 256), BF),
            pltpu.VMEM((4, 4, rows, 256), BF),
            pltpu.VMEM((2, 256, 128), F32),
            pltpu.VMEM((2, 256, 128), F32),
            pltpu.VMEM((NMEM, 4, MEM_DEV, 128), BF),
            pltpu.VMEM((NMEM, 4, MEM_DEV, 128), BF),
            pltpu.VMEM((9, K + 16, 128), BF),
            pltpu.VMEM((4, K, 9 * 128), BF),
            pltpu.VMEM((4, 16, 128), F32),
            pltpu.VMEM((NMEM, 4, MEM_DEV, 128), BF),
            pltpu.VMEM((NMEM, 4, MEM_DEV, 128), BF),
            pltpu.SemaphoreType.DMA((2,)),
            pltpu.SemaphoreType.DMA((2,)),
            pltpu.SemaphoreType.DMA((NMEM,)),
            pltpu.SemaphoreType.DMA((NMEM,)),
            pltpu.SemaphoreType.DMA((9,)),
            pltpu.SemaphoreType.DMA((9,)),
            pltpu.SemaphoreType.DMA((NMEM,)),
            pltpu.SemaphoreType.DMA((NMEM,)),
        ],
        compiler_params=pltpu.CompilerParams(
            collective_id=0, has_side_effects=True, vmem_limit_bytes=48 * 1024 * 1024
        ),
    )(
        ensemble.reshape(MEM_DEV * C, 512),
        conv_first.reshape(2 * 9 * C, HID),
        bias_first,
        conv_second.reshape(2 * 9 * HID, C),
        bias_second,
        observed_cell,
        observed_value,
        observed_precision,
    )
    return result.reshape(MEM_DEV, C, 512)


def solution(mesh):
    in_specs = (
        P("mem", None, "reg"),
        P(),
        P(),
        P(),
        P(),
        P("reg", "mem", None),
        P("reg", "mem", None),
        P("reg", "mem", None),
    )
    out_specs = P("mem", None, "reg")
    return jax.shard_map(body, mesh=mesh, in_specs=in_specs, out_specs=out_specs, check_vma=False)
```

profile of v0, /device:TPU:55, one launch (start us, length us, event | category | flops | bytes accessed | tf_op | source)
XLA Modules:
  0.0 57.9 jit_solution(3380141399133317557)
XLA Ops:
  0.0 0.0 copy-start
  0.0 0.0 copy-start.1
  0.0 0.0 copy-start.2
  0.0 0.0 copy-start.3
  0.0 0.0 copy-start.4
  0.0 0.0 copy-start.6
  0.0 1.0 %copy.9 = bf16[2,9,64,8]{3,2,1,0:T(8,128)(2,1)S(1)} copy(bf16[2,9,64,8]{2,3,1,0:T(8,128)(2,1)} %param.11) | data formatting | bytes 36864 | tf_op args[3]
  1.0 0.0 copy-start.5
  1.0 0.0 copy-done
  1.1 0.0 copy-done.1
  1.1 0.0 copy-done.2
  1.1 0.0 copy-done.3
  1.1 0.0 copy-done.4
  1.1 0.0 copy-done.6
  1.1 0.6 %copy-done.5 = f32[2,64]{1,0:T(2,128)S(1)} copy-done((f32[2,64]{1,0:T(2,128)S(1)}, f32[2,64]{1,0:T(2,128)}, u32[]{:S(2)}) %copy-start.5) | copy-done | bytes 536
  1.7 55.4 %shard_map.82 = bf16[256,512]{1,0:T(8,128)(2,1)S(1)} custom-call(bf16[256,512]{1,0:T(8,128)(2,1)S(1)} %bitcast.6, bf16[144,64]{1,0:T(8,128)(2,1)S(1)} %bitcast.7, f32[2,64]{1,0:T(2,128)S(1)} %copy-done.5, bf16[1152,8]{1,0:T(8,128)(2,1)S(1)} %bitcast.4, f32[2,8]{1,0:T(2,128)S(1)} %copy-done.6, s32[2,2,32]{2,1,0:T(2,128)S(1)} %copy-done.2, ...), custom_call_target="tpu_custom_call" | custom-call | tf_op jit(solution)/shard_map/pallas_call | solution.py:491
  57.2 0.7 %copy.11 = bf16[32,8,512]{2,1,0:T(8,128)(2,1)} copy(bf16[32,8,512]{2,1,0:T(8,128)(2,1)S(1)} %bitcast.5) | data formatting | bytes 524288
Async XLA Ops:
  0.0 1.0 %copy-start = (bf16[32,8,512]{2,1,0:T(8,128)(2,1)S(1)}, bf16[32,8,512]{2,1,0:T(8,128)(2,1)}, u32[]{:S(2)}) copy-start(bf16[32,8,512]{2,1,0:T(8,128)(2,1)} %param.8) | copy-start | bytes 786436
  0.0 1.1 %copy-start.1 = (bf16[2,9,8,64]{3,2,1,0:T(8,128)(2,1)S(1)}, bf16[2,9,8,64]{3,2,1,0:T(8,128)(2,1)}, u32[]{:S(2)}) copy-start(bf16[2,9,8,64]{3,2,1,0:T(8,128)(2,1)} %param.9) | copy-start | bytes 55300
  0.0 1.1 %copy-start.2 = (s32[2,2,32]{2,1,0:T(2,128)S(1)}, s32[2,2,32]{2,1,0:T(2,128)}, u32[]{:S(2)}) copy-start(s32[2,2,32]{2,1,0:T(2,128)} %cell_ref.1) | copy-start | bytes 1540
  0.0 1.1 %copy-start.3 = (f32[2,2,32]{2,1,0:T(2,128)S(1)}, f32[2,2,32]{2,1,0:T(2,128)}, u32[]{:S(2)}) copy-start(f32[2,2,32]{2,1,0:T(2,128)} %value_ref.1) | copy-start | bytes 1540
  0.0 1.1 %copy-start.4 = (f32[2,2,32]{2,1,0:T(2,128)S(1)}, f32[2,2,32]{2,1,0:T(2,128)}, u32[]{:S(2)}) copy-start(f32[2,2,32]{2,1,0:T(2,128)} %prec_ref.1) | copy-start | bytes 1540
  0.0 1.1 %copy-start.6 = (f32[2,8]{1,0:T(2,128)S(1)}, f32[2,8]{1,0:T(2,128)}, u32[]{:S(2)}) copy-start(f32[2,8]{1,0:T(2,128)} %bias_b_ref.1) | copy-start | bytes 196
  1.0 0.7 %copy-start.5 = (f32[2,64]{1,0:T(2,128)S(1)}, f32[2,64]{1,0:T(2,128)}, u32[]{:S(2)}) copy-start(f32[2,64]{1,0:T(2,128)} %bias_a_ref.1) | copy-start | bytes 1540
where the time goes:
time: 58 us; the launch traced here: 57.9 us
  Pallas kernels  55.4 us (96%)
  local copies, waits for them, and re-layouts  2.34 us (4%)
    pallas_call x1, Pallas kernels, body(): pl.pallas_call(kernel, out_shape=jax.ShapeDtypeStruct((MEM_DEV * C, 512),...  55.4 us
    unnamed x16, local copies, waits for them, and re-layouts  2.34 us

commit v1 on v0

--- a/solution.py
+++ b/solution.py
@@ -1,5 +1,3 @@
-import functools
-
 import jax
 import jax.numpy as jnp
 from jax import lax
@@ -99,6 +97,11 @@
     value_ref,
     prec_ref,
     out_ref,
+    rows_of,
+    picker,
+    seen_send,
+    seen_all,
+    seen_side,
     raw,
     w_a,
     w_b,
@@ -122,6 +125,12 @@
     near_recv,
     back_send,
     back_recv,
+    rows_send,
+    rows_recv,
+    seen_send_sem,
+    seen_recv_sem,
+    side_send,
+    side_recv,
 ):
     m = lax.axis_index("mem")
     r = lax.axis_index("reg")
@@ -132,6 +141,14 @@
 
     def peer(d):
         return lax.rem(m + d, NMEM)
+
+    def middle(index):
+        return (index == NMEM // 2 - 1) | (index == NMEM // 2)
+
+    def crosses(dm):
+        if dm == 0:
+            return jnp.bool_(False)
+        return m == (NMEM // 2 - 1 if dm > 0 else NMEM // 2)
 
     for d in range(1, NMEM):
         pl.semaphore_signal(
@@ -184,7 +201,25 @@
         def _(slot=slot):
             near[slot] = jnp.zeros((K + 16, 128), BF)
 
+    def row_of(ref):
+        return jnp.concatenate([ref[t // 2, t % 2 : t % 2 + 1, :] for t in range(4)], axis=1)
+
+    rows_of[m] = jnp.concatenate(
+        [row_of(cell_ref).astype(F32), row_of(value_ref), row_of(prec_ref), jnp.zeros((5, 128), F32)],
+        axis=0,
+    )
+
     pl.semaphore_wait(barrier, arrivals)
+
+    def exchange(d, source, target, send_sem, recv_sem, own=None):
+        return pltpu.make_async_remote_copy(
+            src_ref=source.at[peer(d) if own is None else own],
+            dst_ref=target.at[m],
+            send_sem=send_sem.at[d],
+            recv_sem=recv_sem.at[d],
+            device_id={"mem": peer(d), "reg": r},
+            device_id_type=pl.DeviceIdType.MESH,
+        )
 
     def halo_copy(down):
         return pltpu.make_async_remote_copy(
@@ -204,15 +239,17 @@
     def _():
         halo_copy(False).start()
 
+    rows_copies = [exchange(d, rows_of, rows_of, rows_send, rows_recv, m) for d in range(1, NMEM)]
+    for copy in rows_copies:
+        copy.start()
+
     raw[...] = jnp.zeros(raw.shape, F32)
-    unit = jnp.where(iota((C, C), 0) == iota((C, C), 1), 1.0, 0.0).astype(BF)
     for f in range(2):
         taps = [
             0.5 * first_ref[pl.ds((9 * f + t) * C, C), :].astype(F32) for t in range(9)
         ]
         build_weights(taps, False, raw, 12 * f)
-        turned = dot_nt(unit, second_ref[pl.ds(9 * HID * f, 9 * HID), :])
-        taps = [turned[:, HID * t : HID * t + HID] for t in range(9)]
+        taps = [second_ref[pl.ds((9 * f + t) * C, C), :].astype(F32) for t in range(9)]
         build_weights(taps, True, raw, 12 * f + 6)
         for tile in range(6):
             for side in range(2):
@@ -308,6 +345,12 @@
     for p in range(4):
         field[1, p, 1 : NPC + 1] = branch(0, p, bias_b)
 
+    for copy in rows_copies:
+        copy.wait_recv()
+    for b in range(NMEM):
+        cells = rows_of[b, 0:1, :]
+        picker[b] = jnp.where(iota((128, 128), 0).astype(F32) == cells, 1.0, 0.0).astype(BF)
+
     bias_a, bias_b = biases(1)
     for p in range(4):
         widen(1, p)
@@ -321,42 +364,51 @@
         for ql in range(2):
             send_tiles[:, 2 * (p - 1) + ql] = tiles[:, ql]
 
-    def exchange(d, source, target, send_sem, recv_sem):
+    for b in range(NMEM):
+        found = dot(send_tiles[b].reshape(4 * MEM_DEV, 128), picker[b])
+        seen = found[0:MEM_DEV]
+        for t in range(1, 4):
+            seen = jnp.where(lane // 32 == t, found[MEM_DEV * t : MEM_DEV * t + MEM_DEV], seen)
+        seen_send[b] = seen.astype(BF)
+
+    def side_copy(d):
         return pltpu.make_async_remote_copy(
-            src_ref=source.at[peer(d)],
-            dst_ref=target.at[m],
-            send_sem=send_sem.at[d],
-            recv_sem=recv_sem.at[d],
+            src_ref=seen_send.at[NMEM - 1 - peer(d)],
+            dst_ref=seen_side.at[m],
+            send_sem=side_send.at[d],
+            recv_sem=side_recv.at[d],
             device_id={"mem": peer(d), "reg": r},
             device_id_type=pl.DeviceIdType.MESH,
         )
 
-    tile_copies = [exchange(d, send_tiles, members, tile_send, tile_recv) for d in range(1, NMEM)]
-    for copy in tile_copies:
+    seen_copies = [
+        exchange(d, seen_send, seen_all, seen_send_sem, seen_recv_sem) for d in range(1, NMEM)
+    ]
+    for copy in seen_copies:
         copy.start()
-    members[m] = send_tiles[m]
-    for copy in tile_copies:
+    for d in range(1, NMEM):
+
+        @pl.when(middle(peer(d)))
+        def _(d=d):
+            side_copy(d).start()
+
+    seen_all[m] = seen_send[m]
+    for copy in seen_copies:
         copy.wait_recv()
 
-    def row_of(ref):
-        return jnp.concatenate([ref[t // 2, t % 2 : t % 2 + 1, :] for t in range(4)], axis=1)
-
-    cells = row_of(cell_ref)
-    root = jnp.sqrt(row_of(prec_ref))
-    picker = jnp.where(iota((128, 128), 0) == cells, 1.0, 0.0).astype(BF)
-    seen = jnp.zeros((K, 128), F32)
-    for t in range(4):
-        tile = members[:, t].reshape(K, 128)
-        seen = jnp.where(lane // 32 == t, dot(tile, picker), seen)
-    seen_center = jnp.sum(seen, axis=0, keepdims=True) * (1.0 / K)
-    near[4, 0:K] = ((seen - seen_center) * root).astype(BF)
-    depart = (row_of(value_ref) - seen_center) * root
-    depart_high = depart.astype(BF).astype(F32)
-    depart_low = depart - depart_high
-    sub = iota((16, 128), 0)
-    near[4, K : K + 16] = jnp.where(
-        sub == 0, depart_high, jnp.where(sub == 1, depart_low, 0.0)
-    ).astype(BF)
+    def anomalies(values, owner, slot):
+        seen = values[...].reshape(K, 128).astype(F32)
+        center = jnp.sum(seen, axis=0, keepdims=True) * (1.0 / K)
+        root = jnp.sqrt(rows_of[owner, 2:3, :])
+        near[slot, 0:K] = ((seen - center) * root).astype(BF)
+        depart = (rows_of[owner, 1:2, :] - center) * root
+        high = depart.astype(BF).astype(F32)
+        sub = iota((16, 128), 0)
+        near[slot, K : K + 16] = jnp.where(
+            sub == 0, high, jnp.where(sub == 1, depart - high, 0.0)
+        ).astype(BF)
+
+    anomalies(seen_all, m, 4)
 
     def near_copy(slot):
         dr, dm = NEAR[slot]
@@ -373,20 +425,49 @@
         if slot == 4:
             continue
 
-        @pl.when(inside(dr, dm))
+        @pl.when(inside(dr, dm) & jnp.logical_not(crosses(dm)))
         def _(slot=slot):
             near_copy(slot).start()
 
-    centers = []
-    for t in range(4):
-        tile = members[:, t].reshape(K, 128).astype(F32)
-        centers.append(jnp.sum(tile, axis=0, keepdims=True) * (1.0 / K))
+    def cross_copy(dr, dm):
+        return pltpu.make_async_remote_copy(
+            src_ref=near.at[4 + dm],
+            dst_ref=near.at[3 * (1 - dr) + 1 + dm],
+            send_sem=near_send.at[3 * (1 + dr) + 1 + dm],
+            recv_sem=near_recv.at[3 * (1 - dr) + 1 + dm],
+            device_id={"mem": m, "reg": r + dr},
+            device_id_type=pl.DeviceIdType.MESH,
+        )
+
+    for dm in (-1, 1):
+
+        @pl.when(crosses(dm))
+        def _(dm=dm):
+            seen_side[m] = seen_send[NMEM - 1 - m]
+            for d in range(1, NMEM):
+                side_copy(d).wait_recv()
+            anomalies(seen_side, NMEM - 1 - m, 4 + dm)
+
+        for dr in (-1, 1):
+
+            @pl.when(crosses(dm) & inside(dr, dm))
+            def _(dr=dr, dm=dm):
+                cross_copy(dr, dm).start()
+
+    tile_copies = [exchange(d, send_tiles, members, tile_send, tile_recv) for d in range(1, NMEM)]
+    for copy in tile_copies:
+        copy.start()
+    members[m] = send_tiles[m]
 
     for slot, (dr, dm) in enumerate(NEAR):
         if slot == 4:
             continue
 
-        @pl.when(inside(dr, dm))
+        arrives = inside(dr, dm)
+        if dr == 0:
+            arrives = arrives & jnp.logical_not(crosses(dm))
+
+        @pl.when(arrives)
         def _(slot=slot):
             near_copy(8 - slot).wait_recv()
 
@@ -405,50 +486,71 @@
         both = jnp.concatenate([high, pulls - high], axis=0).astype(BF)
         summed = summed + dot_nt(near[slot, 0:K], both)
 
-    eye = iota((K, K), 0) == iota((K, K), 1)
-    for t in range(4):
-        system = dot_nt(local[t], local[t]) + jnp.where(eye, float(K - 1), 0.0)
-        rows = jnp.sum(jnp.abs(system), axis=0, keepdims=True)
-        bound = jnp.max(rows, axis=1, keepdims=True)
-        scale = 1.0 / bound
-        a_mat = system * scale
-        a_bf = a_mat.astype(BF)
-        y = 1.5 * a_mat - 0.5 * dot(a_bf, a_bf)
+    eye = jnp.where(iota((K, K), 0) == iota((K, K), 1), float(K - 1), 0.0)
+
+    def solve(patches):
+        scale, ys, ds = [], [], []
+        for t in patches:
+            system = dot_nt(local[t], local[t]) + eye
+            rows = jnp.sum(jnp.abs(system), axis=0, keepdims=True)
+            scale.append(1.0 / jnp.max(rows, axis=1, keepdims=True))
+            ds.append(system * scale[-1])
+        lows = [a.astype(BF) for a in ds]
+        ys = [1.5 * a - 0.5 * dot(low, low) for a, low in zip(ds, lows)]
+        ds = [-0.5 * a for a in ds]
         c = 1.5
-        d_mat = -0.5 * a_mat
         for _ in range(2):
-            y_bf = y.astype(BF)
-            d_bf = d_mat.astype(BF)
-            m_mat = c * y + dot(d_bf, y_bf)
-            m_bf = m_mat.astype(BF)
-            y = 1.5 * y - 0.5 * dot(y_bf, m_bf)
-            d_mat = 1.5 * d_mat - (0.5 * c) * m_mat - 0.5 * dot(m_bf, d_bf)
+            y_low = [y.astype(BF) for y in ys]
+            d_low = [d.astype(BF) for d in ds]
+            ms = [c * y + dot(dl, yl) for y, dl, yl in zip(ys, d_low, y_low)]
+            m_low = [mm.astype(BF) for mm in ms]
+            ys = [1.5 * y - 0.5 * dot(yl, ml) for y, yl, ml in zip(ys, y_low, m_low)]
+            ds = [
+                1.5 * d - (0.5 * c) * mm - 0.5 * dot(ml, dl)
+                for d, mm, ml, dl in zip(ds, ms, m_low, d_low)
+            ]
             c = 1.5 * c
-        y_bf = y.astype(BF)
-        d_bf = d_mat.astype(BF)
-        spread = members[:, t].reshape(K, 128).astype(F32) - centers[t]
-        pull = summed[:, t : t + 1] + summed[:, 4 + t : 5 + t]
-        x = jnp.concatenate([spread, jnp.broadcast_to(pull, (K, 128))], axis=1)
-        g = c * x + dot(d_bf, x.astype(BF))
-        h = dot(y_bf, g.astype(BF))
-        g = 1.5 * g - 0.5 * (c * h + dot(d_bf, h.astype(BF)))
-        shift = jnp.sum(g[:, 0:128] * g[:, 128:256], axis=0, keepdims=True) * scale
-        final = centers[t] + shift + jnp.sqrt(float(K - 1) * scale) * g[:, 0:128]
-        send_back[:, t] = final.astype(BF).reshape(NMEM, MEM_DEV, 128)
-
-    back_copies = [exchange(d, send_back, back, back_send, back_recv) for d in range(1, NMEM)]
-    for copy in back_copies:
-        copy.start()
-    back[m] = send_back[m]
-    for copy in back_copies:
-        copy.wait_recv()
+        y_low = [y.astype(BF) for y in ys]
+        d_low = [d.astype(BF) for d in ds]
+        xs = []
+        if patches[0] == 0:
+            for copy in tile_copies:
+                copy.wait_recv()
+        centers = {}
+        for t in patches:
+            tile = members[:, t].reshape(K, 128).astype(F32)
+            centers[t] = jnp.sum(tile, axis=0, keepdims=True) * (1.0 / K)
+            spread = tile - centers[t]
+            pull = summed[:, t : t + 1] + summed[:, 4 + t : 5 + t]
+            xs.append(jnp.concatenate([spread, jnp.broadcast_to(pull, (K, 128))], axis=1))
+        gs = [c * x + dot(dl, x.astype(BF)) for x, dl in zip(xs, d_low)]
+        hs = [dot(yl, g.astype(BF)) for yl, g in zip(y_low, gs)]
+        gs = [
+            1.5 * g - 0.5 * (c * h + dot(dl, h.astype(BF))) for g, h, dl in zip(gs, hs, d_low)
+        ]
+        for t, g, sc in zip(patches, gs, scale):
+            shift = jnp.sum(g[:, 0:128] * g[:, 128:256], axis=0, keepdims=True) * sc
+            final = centers[t] + shift + jnp.sqrt(float(K - 1) * sc) * g[:, 0:128]
+            send_back[t // 2, :, t % 2] = final.astype(BF).reshape(NMEM, MEM_DEV, 128)
+
+    back_copies = []
+    for half in range(2):
+        solve((2 * half, 2 * half + 1))
+        copies = [
+            exchange(d, send_back.at[half], back.at[half], back_send.at[half], back_recv.at[half])
+            for d in range(1, NMEM)
+        ]
+        for copy in copies:
+            copy.start()
+        back[half, m] = send_back[half, m]
+        back_copies.append(copies)
 
     order = cell_order(True)
     for p in range(2):
+        for copy in back_copies[p]:
+            copy.wait_recv()
         for half in range(2):
-            tiles = [
-                back[4 * half + q // 2, 2 * p + q % 2].astype(F32) for q in range(8)
-            ]
+            tiles = [back[p, 4 * half + q // 2, q % 2].astype(F32) for q in range(8)]
             for c, channel in enumerate(block_swap(tiles)):
                 rel_b[half, pl.ds(c, MEM_DEV, stride=C), :] = channel
         cells = jnp.concatenate([rel_b[0], rel_b[1]], axis=1).astype(BF)
@@ -462,18 +564,29 @@
     def _():
         halo_copy(False).wait_send()
 
-    for copy in tile_copies:
+    for copy in rows_copies + seen_copies + tile_copies:
         copy.wait_send()
+    for d in range(1, NMEM):
+
+        @pl.when(middle(peer(d)))
+        def _(d=d):
+            side_copy(d).wait_send()
+
     for slot, (dr, dm) in enumerate(NEAR):
         if slot == 4:
             continue
 
-        @pl.when(inside(dr, dm))
+        leaves = inside(dr, dm)
+        if dr == 0:
+            leaves = leaves & jnp.logical_not(crosses(dm))
+
+        @pl.when(leaves)
         def _(slot=slot):
             near_copy(slot).wait_send()
 
-    for copy in back_copies:
-        copy.wait_send()
+    for copies in back_copies:
+        for copy in copies:
+            copy.wait_send()
 
 
 def body(
@@ -494,6 +607,11 @@
         in_specs=[vmem] * 8,
         out_specs=vmem,
         scratch_shapes=[
+            pltpu.VMEM((NMEM, 8, 128), F32),
+            pltpu.VMEM((NMEM, 128, 128), BF),
+            pltpu.VMEM((NMEM, MEM_DEV, 128), BF),
+            pltpu.VMEM((NMEM, MEM_DEV, 128), BF),
+            pltpu.VMEM((NMEM, MEM_DEV, 128), BF),
             pltpu.VMEM((24, 2, 2, 128, 128), F32),
             pltpu.VMEM((2, 6, 256, 256), BF),
             pltpu.VMEM((2, 6, 256, 256), BF),
@@ -507,14 +625,20 @@
             pltpu.VMEM((9, K + 16, 128), BF),
             pltpu.VMEM((4, K, 9 * 128), BF),
             pltpu.VMEM((4, 16, 128), F32),
-            pltpu.VMEM((NMEM, 4, MEM_DEV, 128), BF),
-            pltpu.VMEM((NMEM, 4, MEM_DEV, 128), BF),
+            pltpu.VMEM((2, NMEM, 2, MEM_DEV, 128), BF),
+            pltpu.VMEM((2, NMEM, 2, MEM_DEV, 128), BF),
             pltpu.SemaphoreType.DMA((2,)),
             pltpu.SemaphoreType.DMA((2,)),
             pltpu.SemaphoreType.DMA((NMEM,)),
             pltpu.SemaphoreType.DMA((NMEM,)),
             pltpu.SemaphoreType.DMA((9,)),
             pltpu.SemaphoreType.DMA((9,)),
+            pltpu.SemaphoreType.DMA((2, NMEM)),
+            pltpu.SemaphoreType.DMA((2, NMEM)),
+            pltpu.SemaphoreType.DMA((NMEM,)),
+            pltpu.SemaphoreType.DMA((NMEM,)),
+            pltpu.SemaphoreType.DMA((NMEM,)),
+            pltpu.SemaphoreType.DMA((NMEM,)),
             pltpu.SemaphoreType.DMA((NMEM,)),
             pltpu.SemaphoreType.DMA((NMEM,)),
         ],
@@ -525,7 +649,7 @@
         ensemble.reshape(MEM_DEV * C, 512),
         conv_first.reshape(2 * 9 * C, HID),
         bias_first,
-        conv_second.reshape(2 * 9 * HID, C),
+        conv_second.transpose(0, 1, 3, 2).reshape(2 * 9 * C, HID),
         bias_second,
         observed_cell,
         observed_value,

time: 58 us -> 55.4 us (0.955)
  the two profiles are of different devices: /device:TPU:55 before, /device:TPU:24 now
where the time goes in v1:
time: 55.4 us; the launch traced here: 55.1 us
  Pallas kernels  49.8 us (90%)
  local copies, waits for them, and re-layouts  5.25 us (9%)
    pallas_call x1, Pallas kernels, body(): pl.pallas_call(kernel, out_shape=jax.ShapeDtypeStruct((MEM_DEV * C, 512),...  49.8 us
    unnamed x17, local copies, waits for them, and re-layouts  5.25 us

profile of v1, /device:TPU:24, one launch (start us, length us, event | category | flops | bytes accessed | tf_op | source)
XLA Modules:
  0.0 55.1 jit_solution(5978953237634752265)
XLA Ops:
  0.0 0.0 copy-start.4
  0.0 0.0 copy-start.3
  0.0 0.0 copy-start.6
  0.0 0.7 %copy-done.4 = f32[2,2,32]{2,1,0:T(2,128)S(1)} copy-done((f32[2,2,32]{2,1,0:T(2,128)S(1)}, f32[2,2,32]{2,1,0:T(2,128)}, u32[]{:S(2)}) %copy-start.4) | copy-done | bytes 536
  0.7 0.0 copy-done.3
  0.7 0.0 copy-done.6
  0.7 0.0 copy-start
  0.7 0.9 %copy-done = bf16[32,8,512]{2,1,0:T(8,128)(2,1)S(1)} copy-done((bf16[32,8,512]{2,1,0:T(8,128)(2,1)S(1)}, bf16[32,8,512]{2,1,0:T(8,128)(2,1)}, u32[]{:S(2)}) %copy-start) | copy-done | bytes 262168
  1.7 0.0 copy-start.1
  1.7 0.8 %copy-done.1 = bf16[2,9,8,64]{3,2,1,0:T(8,128)(2,1)S(1)} copy-done((bf16[2,9,8,64]{3,2,1,0:T(8,128)(2,1)S(1)}, bf16[2,9,8,64]{3,2,1,0:T(8,128)(2,1)}, u32[]{:S(2)}) %copy-start.1) | copy-done | bytes 18456
  2.4 0.0 copy-start.2
  2.4 0.8 %copy-done.2 = bf16[2,9,64,8]{2,3,1,0:T(8,128)(2,1)S(1)} copy-done((bf16[2,9,64,8]{2,3,1,0:T(8,128)(2,1)S(1)}, bf16[2,9,64,8]{2,3,1,0:T(8,128)(2,1)}, u32[]{:S(2)}) %copy-start.2) | copy-done | bytes 18456
  3.2 0.0 copy-start.5
  3.2 0.7 %copy-done.5 = f32[2,2,32]{2,1,0:T(2,128)S(1)} copy-done((f32[2,2,32]{2,1,0:T(2,128)S(1)}, f32[2,2,32]{2,1,0:T(2,128)}, u32[]{:S(2)}) %copy-start.5) | copy-done | bytes 536
  3.9 0.0 copy-start.7
  3.9 0.7 %copy-done.7 = f32[2,8]{1,0:T(2,128)S(1)} copy-done((f32[2,8]{1,0:T(2,128)S(1)}, f32[2,8]{1,0:T(2,128)}, u32[]{:S(2)}) %copy-start.7) | copy-done | bytes 88
  4.6 49.8 %shard_map.82 = bf16[256,512]{1,0:T(8,128)(2,1)S(1)} custom-call(bf16[256,512]{1,0:T(8,128)(2,1)S(1)} %bitcast.7, bf16[144,64]{1,0:T(8,128)(2,1)S(1)} %bitcast.8, f32[2,64]{1,0:T(2,128)S(1)} %copy-done.6, bf16[144,64]{1,0:T(8,128)(2,1)S(1)} %bitcast.9, f32[2,8]{1,0:T(2,128)S(1)} %copy-done.7, s32[2,2,32]{2,1,0:T(2,128)S(1)} %copy-done.3, ...), custom_call_target="tpu_custom_call" | custom-call | tf_op jit(solution)/shard_map/pallas_call | solution.py:604
  54.4 0.7 %copy.10 = bf16[32,8,512]{2,1,0:T(8,128)(2,1)} copy(bf16[32,8,512]{2,1,0:T(8,128)(2,1)S(1)} %bitcast.6) | data formatting | bytes 524288
Async XLA Ops:
  0.0 0.7 %copy-start.4 = (f32[2,2,32]{2,1,0:T(2,128)S(1)}, f32[2,2,32]{2,1,0:T(2,128)}, u32[]{:S(2)}) copy-start(f32[2,2,32]{2,1,0:T(2,128)} %value_ref.1) | copy-start | bytes 1540
  0.0 0.7 %copy-start.3 = (s32[2,2,32]{2,1,0:T(2,128)S(1)}, s32[2,2,32]{2,1,0:T(2,128)}, u32[]{:S(2)}) copy-start(s32[2,2,32]{2,1,0:T(2,128)} %cell_ref.1) | copy-start | bytes 1540
  0.0 0.7 %copy-start.6 = (f32[2,64]{1,0:T(2,128)S(1)}, f32[2,64]{1,0:T(2,128)}, u32[]{:S(2)}) copy-start(f32[2,64]{1,0:T(2,128)} %bias_a_ref.1) | copy-start | bytes 1540
  0.7 0.9 %copy-start = (bf16[32,8,512]{2,1,0:T(8,128)(2,1)S(1)}, bf16[32,8,512]{2,1,0:T(8,128)(2,1)}, u32[]{:S(2)}) copy-start(bf16[32,8,512]{2,1,0:T(8,128)(2,1)} %param.8) | copy-start | bytes 786436
  1.7 0.8 %copy-start.1 = (bf16[2,9,8,64]{3,2,1,0:T(8,128)(2,1)S(1)}, bf16[2,9,8,64]{3,2,1,0:T(8,128)(2,1)}, u32[]{:S(2)}) copy-start(bf16[2,9,8,64]{3,2,1,0:T(8,128)(2,1)} %param.9) | copy-start | bytes 55300
  2.4 0.8 %copy-start.2 = (bf16[2,9,64,8]{2,3,1,0:T(8,128)(2,1)S(1)}, bf16[2,9,64,8]{2,3,1,0:T(8,128)(2,1)}, u32[]{:S(2)}) copy-start(bf16[2,9,64,8]{2,3,1,0:T(8,128)(2,1)} %param.11) | copy-start | bytes 55300
  3.2 0.7 %copy-start.5 = (f32[2,2,32]{2,1,0:T(2,128)S(1)}, f32[2,2,32]{2,1,0:T(2,128)}, u32[]{:S(2)}) copy-start(f32[2,2,32]{2,1,0:T(2,128)} %prec_ref.1) | copy-start | bytes 1540
  3.9 0.7 %copy-start.7 = (f32[2,8]{1,0:T(2,128)S(1)}, f32[2,8]{1,0:T(2,128)}, u32[]{:S(2)}) copy-start(f32[2,8]{1,0:T(2,128)} %bias_b_ref.1) | copy-start | bytes 196

commit v2 on v1

--- a/solution.py
+++ b/solution.py
@@ -88,6 +88,15 @@
 
 
 def kernel(
+    ens_hbm,
+    first_hbm,
+    bias_a_hbm,
+    second_hbm,
+    bias_b_hbm,
+    cell_hbm,
+    value_hbm,
+    prec_hbm,
+    out_ref,
     ens_ref,
     first_ref,
     bias_a_ref,
@@ -96,7 +105,7 @@
     cell_ref,
     value_ref,
     prec_ref,
-    out_ref,
+    load_sem,
     rows_of,
     picker,
     seen_send,
@@ -170,7 +179,26 @@
 
         arrivals = arrivals + jnp.where(inside(dr, dm), 1, 0)
 
+    loads = [
+        pltpu.make_async_copy(source, target, load_sem.at[i])
+        for i, (source, target) in enumerate(
+            (
+                (ens_hbm, ens_ref),
+                (first_hbm, first_ref),
+                (bias_a_hbm, bias_a_ref),
+                (second_hbm, second_ref),
+                (bias_b_hbm, bias_b_ref),
+                (cell_hbm, cell_ref),
+                (value_hbm, value_ref),
+                (prec_hbm, prec_ref),
+            )
+        )
+    ]
+    for load in loads:
+        load.start()
+
     order = cell_order(False)
+    loads[0].wait()
     for p in range(2):
         cells = dot(ens_ref[:, 256 * p : 256 * p + 256], order)
         rel[0] = cells[:, 0:128]
@@ -200,6 +228,9 @@
         @pl.when(jnp.logical_not(inside(dr, dm)))
         def _(slot=slot):
             near[slot] = jnp.zeros((K + 16, 128), BF)
+
+    for load in loads[1:]:
+        load.wait()
 
     def row_of(ref):
         return jnp.concatenate([ref[t // 2, t % 2 : t % 2 + 1, :] for t in range(4)], axis=1)
@@ -392,6 +423,11 @@
         def _(d=d):
             side_copy(d).start()
 
+    tile_copies = [exchange(d, send_tiles, members, tile_send, tile_recv) for d in range(1, NMEM)]
+    for copy in tile_copies:
+        copy.start()
+    members[m] = send_tiles[m]
+
     seen_all[m] = seen_send[m]
     for copy in seen_copies:
         copy.wait_recv()
@@ -453,11 +489,6 @@
             @pl.when(crosses(dm) & inside(dr, dm))
             def _(dr=dr, dm=dm):
                 cross_copy(dr, dm).start()
-
-    tile_copies = [exchange(d, send_tiles, members, tile_send, tile_recv) for d in range(1, NMEM)]
-    for copy in tile_copies:
-        copy.start()
-    members[m] = send_tiles[m]
 
     for slot, (dr, dm) in enumerate(NEAR):
         if slot == 4:
@@ -604,9 +635,18 @@
     result = pl.pallas_call(
         kernel,
         out_shape=jax.ShapeDtypeStruct((MEM_DEV * C, 512), BF),
-        in_specs=[vmem] * 8,
+        in_specs=[pl.BlockSpec(memory_space=pltpu.HBM)] * 8,
         out_specs=vmem,
         scratch_shapes=[
+            pltpu.VMEM((MEM_DEV * C, 512), BF),
+            pltpu.VMEM((2 * 9 * C, HID), BF),
+            pltpu.VMEM((2, HID), F32),
+            pltpu.VMEM((2 * 9 * C, HID), BF),
+            pltpu.VMEM((2, C), F32),
+            pltpu.VMEM((2, 2, 32), jnp.int32),
+            pltpu.VMEM((2, 2, 32), F32),
+            pltpu.VMEM((2, 2, 32), F32),
+            pltpu.SemaphoreType.DMA((8,)),
             pltpu.VMEM((NMEM, 8, 128), F32),
             pltpu.VMEM((NMEM, 128, 128), BF),
             pltpu.VMEM((NMEM, MEM_DEV, 128), BF),
@@ -643,7 +683,7 @@
             pltpu.SemaphoreType.DMA((NMEM,)),
         ],
         compiler_params=pltpu.CompilerParams(
-            collective_id=0, has_side_effects=True, vmem_limit_bytes=48 * 1024 * 1024
+            collective_id=0, has_side_effects=True, vmem_limit_bytes=56 * 1024 * 1024
         ),
     )(
         ensemble.reshape(MEM_DEV * C, 512),

time: 55.4 us -> 50.5 us (0.912)
  local copies, waits for them, and re-layouts: 5.25 us -> 1.67 us
  Pallas kernels: 49.8 us -> 48.7 us
    unnamed x17 -> x1, local copies, waits for them, and re-layouts: 5.25 us -> 1.67 us
    pallas_call x1, Pallas kernels: 49.8 us -> 48.7 us  [body(): pl.pallas_call(kernel, out_shape=jax.ShapeDtypeStruct((MEM_DEV * C, 512),...]
where the time goes in v2:
time: 50.5 us; the launch traced here: 50.4 us
  Pallas kernels  48.7 us (96%)
  local copies, waits for them, and re-layouts  1.67 us (3%)
    pallas_call x1, Pallas kernels, body(): pl.pallas_call(kernel, out_shape=jax.ShapeDtypeStruct((MEM_DEV * C, 512),...  48.7 us
    unnamed x1, local copies, waits for them, and re-layouts  1.67 us

profile of v2, /device:TPU:24, one launch (start us, length us, event | category | flops | bytes accessed | tf_op | source)
XLA Modules:
  0.0 50.4 jit_solution(7880875738652591384)
XLA Ops:
  0.0 48.7 %shard_map.82 = bf16[256,512]{1,0:T(8,128)(2,1)} custom-call(bf16[256,512]{1,0:T(8,128)(2,1)} %bitcast.7, bf16[144,64]{1,0:T(8,128)(2,1)} %bitcast.8, f32[2,64]{1,0:T(2,128)} %bias_a_hbm.1, bf16[144,64]{1,0:T(8,128)(2,1)} %bitcast.9, f32[2,8]{1,0:T(2,128)} %bias_b_hbm.1, s32[2,2,32]{2,1,0:T(2,128)} %cell_hbm.1, f32[2,2,32]{2,1,0:T(2,128)} %value_hbm.1, ...), custom_call_target="tpu_custom_call" | custom-call | tf_op jit(solution)/shard_map/pallas_call | solution.py:635
  48.7 1.7 %copy.10 = bf16[32,8,512]{2,1,0:T(8,128)(2,1)} copy(bf16[32,8,512]{2,1,0:T(8,128)(2,1)} %bitcast.6) | data formatting | bytes 524288

commit v3 on v2

--- a/solution.py
+++ b/solution.py
@@ -117,6 +117,7 @@
     field,
     wide,
     hid,
+    ahead,
     rel,
     rel_b,
     send_tiles,
@@ -207,39 +208,6 @@
             channels = [rel[half, pl.ds(c, MEM_DEV, stride=C), :] for c in range(C)]
             for q, tile in enumerate(block_swap(channels)):
                 field[0, 1 + p, 1 + 8 * half + q] = tile.astype(BF)
-    edge = jnp.zeros((MEM_DEV, 128), BF)
-    for f in range(2):
-        for p in range(4):
-            field[f, p, 0] = edge
-            field[f, p, NPC + 1] = edge
-
-    @pl.when(r == 0)
-    def _():
-        field[0, 0, 1 : NPC + 1] = jnp.zeros((NPC, MEM_DEV, 128), BF)
-
-    @pl.when(r == NREG - 1)
-    def _():
-        field[0, 3, 1 : NPC + 1] = jnp.zeros((NPC, MEM_DEV, 128), BF)
-
-    for slot, (dr, dm) in enumerate(NEAR):
-        if (dr, dm) == (0, 0):
-            continue
-
-        @pl.when(jnp.logical_not(inside(dr, dm)))
-        def _(slot=slot):
-            near[slot] = jnp.zeros((K + 16, 128), BF)
-
-    for load in loads[1:]:
-        load.wait()
-
-    def row_of(ref):
-        return jnp.concatenate([ref[t // 2, t % 2 : t % 2 + 1, :] for t in range(4)], axis=1)
-
-    rows_of[m] = jnp.concatenate(
-        [row_of(cell_ref).astype(F32), row_of(value_ref), row_of(prec_ref), jnp.zeros((5, 128), F32)],
-        axis=0,
-    )
-
     pl.semaphore_wait(barrier, arrivals)
 
     def exchange(d, source, target, send_sem, recv_sem, own=None):
@@ -269,6 +237,39 @@
     @pl.when(r > 0)
     def _():
         halo_copy(False).start()
+
+    edge = jnp.zeros((MEM_DEV, 128), BF)
+    for f in range(2):
+        for p in range(4):
+            field[f, p, 0] = edge
+            field[f, p, NPC + 1] = edge
+
+    @pl.when(r == 0)
+    def _():
+        field[0, 0, 1 : NPC + 1] = jnp.zeros((NPC, MEM_DEV, 128), BF)
+
+    @pl.when(r == NREG - 1)
+    def _():
+        field[0, 3, 1 : NPC + 1] = jnp.zeros((NPC, MEM_DEV, 128), BF)
+
+    for slot, (dr, dm) in enumerate(NEAR):
+        if (dr, dm) == (0, 0):
+            continue
+
+        @pl.when(jnp.logical_not(inside(dr, dm)))
+        def _(slot=slot):
+            near[slot] = jnp.zeros((K + 16, 128), BF)
+
+    for load in loads[1:]:
+        load.wait()
+
+    def row_of(ref):
+        return jnp.concatenate([ref[t // 2, t % 2 : t % 2 + 1, :] for t in range(4)], axis=1)
+
+    rows_of[m] = jnp.concatenate(
+        [row_of(cell_ref).astype(F32), row_of(value_ref), row_of(prec_ref), jnp.zeros((5, 128), F32)],
+        axis=0,
+    )
 
     rows_copies = [exchange(d, rows_of, rows_of, rows_send, rows_recv, m) for d in range(1, NMEM)]
     for copy in rows_copies:
@@ -329,6 +330,9 @@
     def branch(f, p, bias):
         total = None
         terms = [(p, i, i) for i in range(4)] + [(p - 1, 3, TOP), (p + 1, 0, BOTTOM)]
+        if f == 0 and p in (1, 2):
+            total = ahead[p - 1]
+            terms = [(1, 0, 0), (0, 3, TOP)] if p == 1 else [(2, 3, 3), (3, 0, BOTTOM)]
         if p == 0:
             terms = [(0, 1, 1), (0, 2, 2), (0, 3, 3), (1, 0, BOTTOM)]
         if p == 3:
@@ -360,6 +364,15 @@
     widen(0, 2)
     for p, i in ((1, 1), (1, 2), (2, 1), (2, 2), (1, 3), (2, 0)):
         hidden(0, p, i, bias_a)
+    for p, terms in (
+        (1, [(1, 1, 1), (1, 2, 2), (1, 3, 3), (2, 0, BOTTOM)]),
+        (2, [(2, 0, 0), (2, 1, 1), (2, 2, 2), (1, 3, TOP)]),
+    ):
+        total = None
+        for hp, hi, tile in terms:
+            part = dot(hid[hp, hi], w_b[0, tile])
+            total = part if total is None else total + part
+        ahead[p - 1] = total
 
     @pl.when(r < NREG - 1)
     def _():
@@ -393,10 +406,10 @@
     for p in (1, 2):
         tiles = branch(1, p, bias_b).reshape(NMEM, 2, MEM_DEV, 128)
         for ql in range(2):
-            send_tiles[:, 2 * (p - 1) + ql] = tiles[:, ql]
+            send_tiles[p - 1, :, ql] = tiles[:, ql]
 
     for b in range(NMEM):
-        found = dot(send_tiles[b].reshape(4 * MEM_DEV, 128), picker[b])
+        found = dot(send_tiles[:, b].reshape(4 * MEM_DEV, 128), picker[b])
         seen = found[0:MEM_DEV]
         for t in range(1, 4):
             seen = jnp.where(lane // 32 == t, found[MEM_DEV * t : MEM_DEV * t + MEM_DEV], seen)
@@ -423,10 +436,18 @@
         def _(d=d):
             side_copy(d).start()
 
-    tile_copies = [exchange(d, send_tiles, members, tile_send, tile_recv) for d in range(1, NMEM)]
-    for copy in tile_copies:
+    def tile_half(half):
+        return [
+            exchange(
+                d, send_tiles.at[half], members.at[half], tile_send.at[half], tile_recv.at[half]
+            )
+            for d in range(1, NMEM)
+        ]
+
+    tile_copies = [tile_half(0), tile_half(1)]
+    for copy in tile_copies[0] + tile_copies[1]:
         copy.start()
-    members[m] = send_tiles[m]
+    members[:, m] = send_tiles[:, m]
 
     seen_all[m] = seen_send[m]
     for copy in seen_copies:
@@ -457,9 +478,8 @@
             device_id_type=pl.DeviceIdType.MESH,
         )
 
-    for slot, (dr, dm) in enumerate(NEAR):
-        if slot == 4:
-            continue
+    for slot in (0, 2, 6, 8, 1, 7, 3, 5):
+        dr, dm = NEAR[slot]
 
         @pl.when(inside(dr, dm) & jnp.logical_not(crosses(dm)))
         def _(slot=slot):
@@ -490,20 +510,18 @@
             def _(dr=dr, dm=dm):
                 cross_copy(dr, dm).start()
 
-    for slot, (dr, dm) in enumerate(NEAR):
-        if slot == 4:
-            continue
-
-        arrives = inside(dr, dm)
-        if dr == 0:
-            arrives = arrives & jnp.logical_not(crosses(dm))
-
-        @pl.when(arrives)
-        def _(slot=slot):
-            near_copy(8 - slot).wait_recv()
-
     summed = jnp.zeros((K, 8), F32)
-    for slot in range(9):
+    for slot in (4, 3, 5, 1, 7, 0, 2, 6, 8):
+        dr, dm = NEAR[slot]
+        if slot != 4:
+            arrives = inside(dr, dm)
+            if dr == 0:
+                arrives = arrives & jnp.logical_not(crosses(dm))
+
+            @pl.when(arrives)
+            def _(slot=slot):
+                near_copy(8 - slot).wait_recv()
+
         block = near[slot, 0:K].astype(F32)
         tail = near[slot, K : K + 16].astype(F32)
         depart = tail[0:1] + tail[1:2]
@@ -544,12 +562,11 @@
         y_low = [y.astype(BF) for y in ys]
         d_low = [d.astype(BF) for d in ds]
         xs = []
-        if patches[0] == 0:
-            for copy in tile_copies:
-                copy.wait_recv()
+        for copy in tile_copies[patches[0] // 2]:
+            copy.wait_recv()
         centers = {}
         for t in patches:
-            tile = members[:, t].reshape(K, 128).astype(F32)
+            tile = members[t // 2, :, t % 2].reshape(K, 128).astype(F32)
             centers[t] = jnp.sum(tile, axis=0, keepdims=True) * (1.0 / K)
             spread = tile - centers[t]
             pull = summed[:, t : t + 1] + summed[:, 4 + t : 5 + t]
@@ -595,7 +612,7 @@
     def _():
         halo_copy(False).wait_send()
 
-    for copy in rows_copies + seen_copies + tile_copies:
+    for copy in rows_copies + seen_copies + tile_copies[0] + tile_copies[1]:
         copy.wait_send()
     for d in range(1, NMEM):
 
@@ -658,10 +675,11 @@
             pltpu.VMEM((2, 4, NPC + 2, MEM_DEV, 128), BF),
             pltpu.VMEM((4, rows, 256), BF),
             pltpu.VMEM((4, 4, rows, 256), BF),
+            pltpu.VMEM((2, rows, 256), F32),
             pltpu.VMEM((2, 256, 128), F32),
             pltpu.VMEM((2, 256, 128), F32),
-            pltpu.VMEM((NMEM, 4, MEM_DEV, 128), BF),
-            pltpu.VMEM((NMEM, 4, MEM_DEV, 128), BF),
+            pltpu.VMEM((2, NMEM, 2, MEM_DEV, 128), BF),
+            pltpu.VMEM((2, NMEM, 2, MEM_DEV, 128), BF),
             pltpu.VMEM((9, K + 16, 128), BF),
             pltpu.VMEM((4, K, 9 * 128), BF),
             pltpu.VMEM((4, 16, 128), F32),
@@ -669,8 +687,8 @@
             pltpu.VMEM((2, NMEM, 2, MEM_DEV, 128), BF),
             pltpu.SemaphoreType.DMA((2,)),
             pltpu.SemaphoreType.DMA((2,)),
-            pltpu.SemaphoreType.DMA((NMEM,)),
-            pltpu.SemaphoreType.DMA((NMEM,)),
+            pltpu.SemaphoreType.DMA((2, NMEM)),
+            pltpu.SemaphoreType.DMA((2, NMEM)),
             pltpu.SemaphoreType.DMA((9,)),
             pltpu.SemaphoreType.DMA((9,)),
             pltpu.SemaphoreType.DMA((2, NMEM)),

time: 50.5 us -> 50.5 us (level); the launches traced: 50.4 us -> 49.8 us
    pallas_call x1, Pallas kernels: 48.7 us -> 48.2 us  [body(): pl.pallas_call(kernel, out_shape=jax.ShapeDtypeStruct((MEM_DEV * C, 512),...]
where the time goes in v3:
time: 50.5 us; the launch traced here: 49.8 us
  Pallas kernels  48.2 us (95%)
  local copies, waits for them, and re-layouts  1.67 us (3%)
    pallas_call x1, Pallas kernels, body(): pl.pallas_call(kernel, out_shape=jax.ShapeDtypeStruct((MEM_DEV * C, 512),...  48.2 us
    unnamed x1, local copies, waits for them, and re-layouts  1.67 us

profile of v3, /device:TPU:24, one launch (start us, length us, event | category | flops | bytes accessed | tf_op | source)
XLA Modules:
  0.0 49.8 jit_solution(7460063409500706502)
XLA Ops:
  0.0 48.2 %shard_map.82 = bf16[256,512]{1,0:T(8,128)(2,1)} custom-call(bf16[256,512]{1,0:T(8,128)(2,1)} %bitcast.7, bf16[144,64]{1,0:T(8,128)(2,1)} %bitcast.8, f32[2,64]{1,0:T(2,128)} %bias_a_hbm.1, bf16[144,64]{1,0:T(8,128)(2,1)} %bitcast.9, f32[2,8]{1,0:T(2,128)} %bias_b_hbm.1, s32[2,2,32]{2,1,0:T(2,128)} %cell_hbm.1, f32[2,2,32]{2,1,0:T(2,128)} %value_hbm.1, ...), custom_call_target="tpu_custom_call" | custom-call | tf_op jit(solution)/shard_map/pallas_call | solution.py:652
  48.2 1.7 %copy.10 = bf16[32,8,512]{2,1,0:T(8,128)(2,1)} copy(bf16[32,8,512]{2,1,0:T(8,128)(2,1)} %bitcast.6) | data formatting | bytes 524288
